TPU v7x, 128 devices: a whole 4x4x4 slice. The times are simulated.
128 devices in a mesh: layer: 4 (over z), leaf: 32 (over x, y, core).
Axes of the slice: x: 4, y: 4, z: 4, core: 2. Of those that a mesh axis runs over, the one named last changes fastest.
Arguments:
- sources: float32 [2, 4, 32, 384, 256], P(None, 'layer', 'leaf'), may hold values from -6 to 6
- leaf_inverse: float32 [2, 4, 32, 384, 384], P(None, 'layer', 'leaf'), may hold values from -0.21875 to 0.21875
- tree_up: float32 [2, 4, 32, 5, 384, 384], P(None, 'layer', 'leaf'), may hold values from -0.0546875 to 0.0546875
- tree_down: float32 [2, 4, 32, 5, 384, 384], P(None, 'layer', 'leaf'), may hold values from -0.0546875 to 0.0546875
- coupling: float32 [2, 4, 32, 384, 128], P(None, 'layer', 'leaf'), may hold values from -0.1875 to 0.1875
- index_map: int32 [4, 32, 384], P('layer', 'leaf'), may hold values from 0 to 383, each once within a row
Outputs:
- solution: float32 [2, 4, 32, 384, 256], P(None, 'layer', 'leaf')
Inputs may be any that keep to these rules, and one draw needn't show every extreme that they name: `index_map`: each row of the last dimension holds every number from 0 to 383 once.
All inputs are finite; a program needn't handle non-finite values.
Results may differ from a plain program's by a relative error of at most 0.0001.
Values sent between devices are 32-bit elements; how exact they have to be, the bound alone decides.
A program may use at most 128 MiB of HBM per device.

v0:
```python
import jax
import jax.numpy as jnp
from jax import lax
from jax.sharding import PartitionSpec as P


def from_behind(x, axis, by):
    size = lax.axis_size(axis)
    pairs = [(i, i + by) for i in range(size) if 0 <= i + by < size]
    return lax.ppermute(x, axis, pairs)


def swapped(block, axis, stride):
    count = lax.axis_size(axis)
    route = []
    for low in range(count):
        high = low | 1 << stride
        if high != low and high < count:
            route += [(low, high), (high, low)]
    return lax.ppermute(block, axis, route)


def complex_apply(matrix, vector):
    highest = lax.Precision.HIGHEST
    real_real = jnp.matmul(matrix[0], vector[0], precision=highest)
    imag_imag = jnp.matmul(matrix[1], vector[1], precision=highest)
    real_imag = jnp.matmul(matrix[0], vector[1], precision=highest)
    imag_real = jnp.matmul(matrix[1], vector[0], precision=highest)
    return jnp.stack([real_real - imag_imag, real_imag + imag_real])


def per_device(sources, leaf_inverse, tree_up, tree_down, coupling, index_map):
    front_size = leaf_inverse.shape[-1]
    all_columns = sources.shape[-1]
    tree_levels = lax.axis_size("leaf").bit_length() - 1
    layer_count = lax.axis_size("layer")
    my_layer = lax.axis_index("layer")
    sources_local = sources.reshape(2, front_size, all_columns)
    inverse_local = leaf_inverse.reshape(2, front_size, front_size)
    upward = tree_up.reshape(2, tree_levels, front_size, front_size)
    downward = tree_down.reshape(2, tree_levels, front_size, front_size)
    coupling_local = coupling.reshape(2, front_size, coupling.shape[-1])
    border_rows = coupling_local.shape[-1]
    front_order = index_map.reshape(front_size)
    front_undo = jnp.argsort(front_order)
    block_count = 1
    block_width = all_columns // block_count
    solution = jnp.zeros_like(sources_local)
    outgoing = jnp.zeros((2, border_rows, block_width), jnp.float32)
    for section_step in range(block_count + layer_count - 1):
        incoming = from_behind(outgoing, "layer", 1)
        block_index = section_step - my_layer
        is_live = jnp.logical_and(block_index >= 0, block_index < block_count)
        reduced = sources_local - complex_apply(coupling_local, incoming)
        frontal = complex_apply(inverse_local, reduced[:, front_order, :])
        for tree_bit in range(tree_levels):
            mirrored = swapped(frontal, "leaf", tree_bit)
            frontal = frontal + complex_apply(upward[:, tree_bit], mirrored)
        for tree_bit in reversed(range(tree_levels)):
            mirrored = swapped(frontal, "leaf", tree_bit)
            frontal = frontal + complex_apply(downward[:, tree_bit], mirrored)
        solved = frontal[:, front_undo, :]
        current = solution
        solution = jnp.where(is_live, solved, current)
        outgoing = solved[:, front_size - border_rows :, :]
    return solution.reshape(sources.shape)


def solution(mesh):
    placed = (
        P(None, "layer", "leaf", None, None),
        P(None, "layer", "leaf", None, None),
        P(None, "layer", "leaf", None, None, None),
        P(None, "layer", "leaf", None, None, None),
        P(None, "layer", "leaf", None, None),
        P("layer", "leaf", None),
    )
    return jax.shard_map(
        per_device,
        mesh=mesh,
        in_specs=placed,
        out_specs=P(None, "layer", "leaf", None, None),
        check_vma=False,
    )
```

profile of v0, /device:TPU:97, one launch (start us, length us, event | category | flops | bytes accessed | tf_op | source)
XLA Modules:
  0.0 894.8 jit_solution(10898935808135540693)
XLA Ops:
  40.6 17.5 %collective-permute-done.2 = f32[2,384,256]{1,2,0:T(8,128)S(1)} collective-permute-done((f32[2,384,256]{1,2,0:T(8,128)S(1)}, f32[2,384,256]{1,2,0:T(8,128)S(1)}, u32[]{:S(2)}, u32[]{:S(2)}) %collective-permute-start.2) | collective-permute-done | bytes 786464 | tf_op jit(solution)/shard_map/ppermute | solution.py:20
  65.3 16.4 %collective-permute-done.3 = f32[2,384,256]{1,2,0:T(8,128)S(1)} collective-permute-done((f32[2,384,256]{1,2,0:T(8,128)S(1)}, f32[2,384,256]{1,2,0:T(8,128)S(1)}, u32[]{:S(2)}, u32[]{:S(2)}) %collective-permute-start.3) | collective-permute-done | bytes 786464 | tf_op jit(solution)/shard_map/ppermute | solution.py:20
  86.9 15.7 %collective-permute-done.4 = f32[2,384,256]{1,2,0:T(8,128)S(1)} collective-permute-done((f32[2,384,256]{1,2,0:T(8,128)S(1)}, f32[2,384,256]{1,2,0:T(8,128)S(1)}, u32[]{:S(2)}, u32[]{:S(2)}) %collective-permute-start.4) | collective-permute-done | bytes 786464 | tf_op jit(solution)/shard_map/ppermute | solution.py:20
  109.5 14.7 %collective-permute-done.5 = f32[2,384,256]{1,2,0:T(8,128)S(1)} collective-permute-done((f32[2,384,256]{1,2,0:T(8,128)S(1)}, f32[2,384,256]{1,2,0:T(8,128)S(1)}, u32[]{:S(2)}, u32[]{:S(2)}) %collective-permute-start.5) | collective-permute-done | bytes 786464 | tf_op jit(solution)/shard_map/ppermute | solution.py:20
  131.0 13.8 %collective-permute-done.6 = f32[2,384,256]{1,2,0:T(8,128)S(1)} collective-permute-done((f32[2,384,256]{1,2,0:T(8,128)S(1)}, f32[2,384,256]{1,2,0:T(8,128)S(1)}, u32[]{:S(2)}, u32[]{:S(2)}) %collective-permute-start.6) | collective-permute-done | bytes 786464 | tf_op jit(solution)/shard_map/ppermute | solution.py:20
  150.4 12.9 %collective-permute-done.7 = f32[2,384,256]{1,2,0:T(8,128)S(1)} collective-permute-done((f32[2,384,256]{1,2,0:T(8,128)S(1)}, f32[2,384,256]{1,2,0:T(8,128)S(1)}, u32[]{:S(2)}, u32[]{:S(2)}) %collective-permute-start.7) | collective-permute-done | bytes 786464 | tf_op jit(solution)/shard_map/ppermute | solution.py:20
  271.0 17.5 %collective-permute-done.13 = f32[2,384,256]{1,2,0:T(8,128)S(1)} collective-permute-done((f32[2,384,256]{1,2,0:T(8,128)S(1)}, f32[2,384,256]{1,2,0:T(8,128)S(1)}, u32[]{:S(2)}, u32[]{:S(2)}) %collective-permute-start.13) | collective-permute-done | bytes 786464 | tf_op jit(solution)/shard_map/ppermute | solution.py:20
  295.6 16.4 %collective-permute-done.14 = f32[2,384,256]{1,2,0:T(8,128)S(1)} collective-permute-done((f32[2,384,256]{1,2,0:T(8,128)S(1)}, f32[2,384,256]{1,2,0:T(8,128)S(1)}, u32[]{:S(2)}, u32[]{:S(2)}) %collective-permute-start.14) | collective-permute-done | bytes 786464 | tf_op jit(solution)/shard_map/ppermute | solution.py:20
  317.2 15.7 %collective-permute-done.15 = f32[2,384,256]{1,2,0:T(8,128)S(1)} collective-permute-done((f32[2,384,256]{1,2,0:T(8,128)S(1)}, f32[2,384,256]{1,2,0:T(8,128)S(1)}, u32[]{:S(2)}, u32[]{:S(2)}) %collective-permute-start.15) | collective-permute-done | bytes 786464 | tf_op jit(solution)/shard_map/ppermute | solution.py:20
  339.8 14.7 %collective-permute-done.16 = f32[2,384,256]{1,2,0:T(8,128)S(1)} collective-permute-done((f32[2,384,256]{1,2,0:T(8,128)S(1)}, f32[2,384,256]{1,2,0:T(8,128)S(1)}, u32[]{:S(2)}, u32[]{:S(2)}) %collective-permute-start.16) | collective-permute-done | bytes 786464 | tf_op jit(solution)/shard_map/ppermute | solution.py:20
  361.4 13.8 %collective-permute-done.17 = f32[2,384,256]{1,2,0:T(8,128)S(1)} collective-permute-done((f32[2,384,256]{1,2,0:T(8,128)S(1)}, f32[2,384,256]{1,2,0:T(8,128)S(1)}, u32[]{:S(2)}, u32[]{:S(2)}) %collective-permute-start.17) | collective-permute-done | bytes 786464 | tf_op jit(solution)/shard_map/ppermute | solution.py:20
  380.6 12.9 %collective-permute-done.18 = f32[2,384,256]{1,2,0:T(8,128)S(1)} collective-permute-done((f32[2,384,256]{1,2,0:T(8,128)S(1)}, f32[2,384,256]{1,2,0:T(8,128)S(1)}, u32[]{:S(2)}, u32[]{:S(2)}) %collective-permute-start.18) | collective-permute-done | bytes 786464 | tf_op jit(solution)/shard_map/ppermute | solution.py:20
  487.2 17.4 %collective-permute-done.24 = f32[2,384,256]{1,2,0:T(8,128)S(1)} collective-permute-done((f32[2,384,256]{1,2,0:T(8,128)S(1)}, f32[2,384,256]{1,2,0:T(8,128)S(1)}, u32[]{:S(2)}, u32[]{:S(2)}) %collective-permute-start.24) | collective-permute-done | bytes 786464 | tf_op jit(solution)/shard_map/ppermute | solution.py:20
  511.9 16.4 %collective-permute-done.25 = f32[2,384,256]{1,2,0:T(8,128)S(1)} collective-permute-done((f32[2,384,256]{1,2,0:T(8,128)S(1)}, f32[2,384,256]{1,2,0:T(8,128)S(1)}, u32[]{:S(2)}, u32[]{:S(2)}) %collective-permute-start.25) | collective-permute-done | bytes 786464 | tf_op jit(solution)/shard_map/ppermute | solution.py:20
  533.4 15.7 %collective-permute-done.26 = f32[2,384,256]{1,2,0:T(8,128)S(1)} collective-permute-done((f32[2,384,256]{1,2,0:T(8,128)S(1)}, f32[2,384,256]{1,2,0:T(8,128)S(1)}, u32[]{:S(2)}, u32[]{:S(2)}) %collective-permute-start.26) | collective-permute-done | bytes 786464 | tf_op jit(solution)/shard_map/ppermute | solution.py:20
  556.1 14.7 %collective-permute-done.27 = f32[2,384,256]{1,2,0:T(8,128)S(1)} collective-permute-done((f32[2,384,256]{1,2,0:T(8,128)S(1)}, f32[2,384,256]{1,2,0:T(8,128)S(1)}, u32[]{:S(2)}, u32[]{:S(2)}) %collective-permute-start.27) | collective-permute-done | bytes 786464 | tf_op jit(solution)/shard_map/ppermute | solution.py:20
  577.6 13.8 %collective-permute-done.28 = f32[2,384,256]{1,2,0:T(8,128)S(1)} collective-permute-done((f32[2,384,256]{1,2,0:T(8,128)S(1)}, f32[2,384,256]{1,2,0:T(8,128)S(1)}, u32[]{:S(2)}, u32[]{:S(2)}) %collective-permute-start.28) | collective-permute-done | bytes 786464 | tf_op jit(solution)/shard_map/ppermute | solution.py:20
  596.9 12.9 %collective-permute-done.29 = f32[2,384,256]{1,2,0:T(8,128)S(1)} collective-permute-done((f32[2,384,256]{1,2,0:T(8,128)S(1)}, f32[2,384,256]{1,2,0:T(8,128)S(1)}, u32[]{:S(2)}, u32[]{:S(2)}) %collective-permute-start.29) | collective-permute-done | bytes 786464 | tf_op jit(solution)/shard_map/ppermute | solution.py:20
  703.5 17.4 %collective-permute-done.35 = f32[2,384,256]{1,2,0:T(8,128)S(1)} collective-permute-done((f32[2,384,256]{1,2,0:T(8,128)S(1)}, f32[2,384,256]{1,2,0:T(8,128)S(1)}, u32[]{:S(2)}, u32[]{:S(2)}) %collective-permute-start.35) | collective-permute-done | bytes 786464 | tf_op jit(solution)/shard_map/ppermute | solution.py:20
  728.2 16.4 %collective-permute-done.36 = f32[2,384,256]{1,2,0:T(8,128)S(1)} collective-permute-done((f32[2,384,256]{1,2,0:T(8,128)S(1)}, f32[2,384,256]{1,2,0:T(8,128)S(1)}, u32[]{:S(2)}, u32[]{:S(2)}) %collective-permute-start.36) | collective-permute-done | bytes 786464 | tf_op jit(solution)/shard_map/ppermute | solution.py:20
  749.8 15.7 %collective-permute-done.37 = f32[2,384,256]{1,2,0:T(8,128)S(1)} collective-permute-done((f32[2,384,256]{1,2,0:T(8,128)S(1)}, f32[2,384,256]{1,2,0:T(8,128)S(1)}, u32[]{:S(2)}, u32[]{:S(2)}) %collective-permute-start.37) | collective-permute-done | bytes 786464 | tf_op jit(solution)/shard_map/ppermute | solution.py:20
  772.5 14.7 %collective-permute-done.38 = f32[2,384,256]{1,2,0:T(8,128)S(1)} collective-permute-done((f32[2,384,256]{1,2,0:T(8,128)S(1)}, f32[2,384,256]{1,2,0:T(8,128)S(1)}, u32[]{:S(2)}, u32[]{:S(2)}) %collective-permute-start.38) | collective-permute-done | bytes 786464 | tf_op jit(solution)/shard_map/ppermute | solution.py:20
  794.0 13.8 %collective-permute-done.39 = f32[2,384,256]{1,2,0:T(8,128)S(1)} collective-permute-done((f32[2,384,256]{1,2,0:T(8,128)S(1)}, f32[2,384,256]{1,2,0:T(8,128)S(1)}, u32[]{:S(2)}, u32[]{:S(2)}) %collective-permute-start.39) | collective-permute-done | bytes 786464 | tf_op jit(solution)/shard_map/ppermute | solution.py:20
  813.3 13.0 %collective-permute-done.40 = f32[2,384,256]{1,2,0:T(8,128)S(1)} collective-permute-done((f32[2,384,256]{1,2,0:T(8,128)S(1)}, f32[2,384,256]{1,2,0:T(8,128)S(1)}, u32[]{:S(2)}, u32[]{:S(2)}) %collective-permute-start.40) | collective-permute-done | bytes 786464 | tf_op jit(solution)/shard_map/ppermute | solution.py:20
  (527 shorter events, 527.3 us)
Async XLA Ops:
  39.2 18.8 %collective-permute-start.2 = (f32[2,384,256]{1,2,0:T(8,128)S(1)}, f32[2,384,256]{1,2,0:T(8,128)S(1)}, u32[]{:S(2)}, u32[]{:S(2)}) collective-permute-start(f32[2,384,256]{1,2,0:T(8,128)S(1)} %maximum_add_fusion), channel_id=1, source_target_pairs={{0,2},{2,0},{1,3},{3,1},{4,6},{6,4},{5,7},{7,5},{8,10},{10,8},{9,1... | collective-permute-start | bytes 2359304 | tf_op jit(solution)/shard_map/ppermute | solution.py:20
  61.9 19.8 %collective-permute-start.3 = (f32[2,384,256]{1,2,0:T(8,128)S(1)}, f32[2,384,256]{1,2,0:T(8,128)S(1)}, u32[]{:S(2)}, u32[]{:S(2)}) collective-permute-start(f32[2,384,256]{1,2,0:T(8,128)S(1)} %maximum_add_fusion.1), channel_id=1, source_target_pairs={{0,4},{4,0},{1,5},{5,1},{2,6},{6,2},{3,7},{7,3},{8,12},{12,8},{9,1... | collective-permute-start | bytes 2359304 | tf_op jit(solution)/shard_map/ppermute | solution.py:20
  85.6 17.0 %collective-permute-start.4 = (f32[2,384,256]{1,2,0:T(8,128)S(1)}, f32[2,384,256]{1,2,0:T(8,128)S(1)}, u32[]{:S(2)}, u32[]{:S(2)}) collective-permute-start(f32[2,384,256]{1,2,0:T(8,128)S(1)} %maximum_add_fusion.2), channel_id=1, source_target_pairs={{0,8},{8,0},{1,9},{9,1},{2,10},{10,2},{3,11},{11,3},{4,12},{12,4},... | collective-permute-start | bytes 2359304 | tf_op jit(solution)/shard_map/ppermute | solution.py:20
  106.5 17.7 %collective-permute-start.5 = (f32[2,384,256]{1,2,0:T(8,128)S(1)}, f32[2,384,256]{1,2,0:T(8,128)S(1)}, u32[]{:S(2)}, u32[]{:S(2)}) collective-permute-start(f32[2,384,256]{1,2,0:T(8,128)S(1)} %maximum_add_fusion.3), channel_id=1, source_target_pairs={{0,16},{16,0},{1,17},{17,1},{2,18},{18,2},{3,19},{19,3},{4,20},{20... | collective-permute-start | bytes 2359304 | tf_op jit(solution)/shard_map/ppermute | solution.py:20
  128.2 16.7 %collective-permute-start.6 = (f32[2,384,256]{1,2,0:T(8,128)S(1)}, f32[2,384,256]{1,2,0:T(8,128)S(1)}, u32[]{:S(2)}, u32[]{:S(2)}) collective-permute-start(f32[2,384,256]{1,2,0:T(8,128)S(1)} %maximum_add_fusion.4), channel_id=1, source_target_pairs={{0,16},{16,0},{1,17},{17,1},{2,18},{18,2},{3,19},{19,3},{4,20},{20... | collective-permute-start | bytes 2359304 | tf_op jit(solution)/shard_map/ppermute | solution.py:20
  167.3 14.8 %collective-permute-start.8 = (f32[2,384,256]{1,2,0:T(8,128)S(1)}, f32[2,384,256]{1,2,0:T(8,128)S(1)}, u32[]{:S(2)}, u32[]{:S(2)}) collective-permute-start(f32[2,384,256]{1,2,0:T(8,128)S(1)} %maximum_add_fusion.6), channel_id=1, source_target_pairs={{0,4},{4,0},{1,5},{5,1},{2,6},{6,2},{3,7},{7,3},{8,12},{12,8},{9,1... | collective-permute-start | bytes 2359304 | tf_op jit(solution)/shard_map/ppermute | solution.py:20
  269.6 18.8 %collective-permute-start.13 = (f32[2,384,256]{1,2,0:T(8,128)S(1)}, f32[2,384,256]{1,2,0:T(8,128)S(1)}, u32[]{:S(2)}, u32[]{:S(2)}) collective-permute-start(f32[2,384,256]{1,2,0:T(8,128)S(1)} %maximum_add_fusion.10), channel_id=1, source_target_pairs={{0,2},{2,0},{1,3},{3,1},{4,6},{6,4},{5,7},{7,5},{8,10},{10,8},{9,1... | collective-permute-start | bytes 2359304 | tf_op jit(solution)/shard_map/ppermute | solution.py:20
  292.2 19.8 %collective-permute-start.14 = (f32[2,384,256]{1,2,0:T(8,128)S(1)}, f32[2,384,256]{1,2,0:T(8,128)S(1)}, u32[]{:S(2)}, u32[]{:S(2)}) collective-permute-start(f32[2,384,256]{1,2,0:T(8,128)S(1)} %maximum_add_fusion.11), channel_id=1, source_target_pairs={{0,4},{4,0},{1,5},{5,1},{2,6},{6,2},{3,7},{7,3},{8,12},{12,8},{9,1... | collective-permute-start | bytes 2359304 | tf_op jit(solution)/shard_map/ppermute | solution.py:20
  315.9 17.0 %collective-permute-start.15 = (f32[2,384,256]{1,2,0:T(8,128)S(1)}, f32[2,384,256]{1,2,0:T(8,128)S(1)}, u32[]{:S(2)}, u32[]{:S(2)}) collective-permute-start(f32[2,384,256]{1,2,0:T(8,128)S(1)} %maximum_add_fusion.12), channel_id=1, source_target_pairs={{0,8},{8,0},{1,9},{9,1},{2,10},{10,2},{3,11},{11,3},{4,12},{12,4},... | collective-permute-start | bytes 2359304 | tf_op jit(solution)/shard_map/ppermute | solution.py:20
  336.8 17.7 %collective-permute-start.16 = (f32[2,384,256]{1,2,0:T(8,128)S(1)}, f32[2,384,256]{1,2,0:T(8,128)S(1)}, u32[]{:S(2)}, u32[]{:S(2)}) collective-permute-start(f32[2,384,256]{1,2,0:T(8,128)S(1)} %maximum_add_fusion.13), channel_id=1, source_target_pairs={{0,16},{16,0},{1,17},{17,1},{2,18},{18,2},{3,19},{19,3},{4,20},{20... | collective-permute-start | bytes 2359304 | tf_op jit(solution)/shard_map/ppermute | solution.py:20
  358.5 16.6 %collective-permute-start.17 = (f32[2,384,256]{1,2,0:T(8,128)S(1)}, f32[2,384,256]{1,2,0:T(8,128)S(1)}, u32[]{:S(2)}, u32[]{:S(2)}) collective-permute-start(f32[2,384,256]{1,2,0:T(8,128)S(1)} %maximum_add_fusion.14), channel_id=1, source_target_pairs={{0,16},{16,0},{1,17},{17,1},{2,18},{18,2},{3,19},{19,3},{4,20},{20... | collective-permute-start | bytes 2359304 | tf_op jit(solution)/shard_map/ppermute | solution.py:20
  397.6 14.8 %collective-permute-start.19 = (f32[2,384,256]{1,2,0:T(8,128)S(1)}, f32[2,384,256]{1,2,0:T(8,128)S(1)}, u32[]{:S(2)}, u32[]{:S(2)}) collective-permute-start(f32[2,384,256]{1,2,0:T(8,128)S(1)} %maximum_add_fusion.16), channel_id=1, source_target_pairs={{0,4},{4,0},{1,5},{5,1},{2,6},{6,2},{3,7},{7,3},{8,12},{12,8},{9,1... | collective-permute-start | bytes 2359304 | tf_op jit(solution)/shard_map/ppermute | solution.py:20
  485.8 18.8 %collective-permute-start.24 = (f32[2,384,256]{1,2,0:T(8,128)S(1)}, f32[2,384,256]{1,2,0:T(8,128)S(1)}, u32[]{:S(2)}, u32[]{:S(2)}) collective-permute-start(f32[2,384,256]{1,2,0:T(8,128)S(1)} %maximum_add_fusion.20), channel_id=1, source_target_pairs={{0,2},{2,0},{1,3},{3,1},{4,6},{6,4},{5,7},{7,5},{8,10},{10,8},{9,1... | collective-permute-start | bytes 2359304 | tf_op jit(solution)/shard_map/ppermute | solution.py:20
  508.4 19.8 %collective-permute-start.25 = (f32[2,384,256]{1,2,0:T(8,128)S(1)}, f32[2,384,256]{1,2,0:T(8,128)S(1)}, u32[]{:S(2)}, u32[]{:S(2)}) collective-permute-start(f32[2,384,256]{1,2,0:T(8,128)S(1)} %maximum_add_fusion.21), channel_id=1, source_target_pairs={{0,4},{4,0},{1,5},{5,1},{2,6},{6,2},{3,7},{7,3},{8,12},{12,8},{9,1... | collective-permute-start | bytes 2359304 | tf_op jit(solution)/shard_map/ppermute | solution.py:20
  532.1 17.0 %collective-permute-start.26 = (f32[2,384,256]{1,2,0:T(8,128)S(1)}, f32[2,384,256]{1,2,0:T(8,128)S(1)}, u32[]{:S(2)}, u32[]{:S(2)}) collective-permute-start(f32[2,384,256]{1,2,0:T(8,128)S(1)} %maximum_add_fusion.22), channel_id=1, source_target_pairs={{0,8},{8,0},{1,9},{9,1},{2,10},{10,2},{3,11},{11,3},{4,12},{12,4},... | collective-permute-start | bytes 2359304 | tf_op jit(solution)/shard_map/ppermute | solution.py:20
  553.0 17.7 %collective-permute-start.27 = (f32[2,384,256]{1,2,0:T(8,128)S(1)}, f32[2,384,256]{1,2,0:T(8,128)S(1)}, u32[]{:S(2)}, u32[]{:S(2)}) collective-permute-start(f32[2,384,256]{1,2,0:T(8,128)S(1)} %maximum_add_fusion.23), channel_id=1, source_target_pairs={{0,16},{16,0},{1,17},{17,1},{2,18},{18,2},{3,19},{19,3},{4,20},{20... | collective-permute-start | bytes 2359304 | tf_op jit(solution)/shard_map/ppermute | solution.py:20
  574.7 16.6 %collective-permute-start.28 = (f32[2,384,256]{1,2,0:T(8,128)S(1)}, f32[2,384,256]{1,2,0:T(8,128)S(1)}, u32[]{:S(2)}, u32[]{:S(2)}) collective-permute-start(f32[2,384,256]{1,2,0:T(8,128)S(1)} %maximum_add_fusion.24), channel_id=1, source_target_pairs={{0,16},{16,0},{1,17},{17,1},{2,18},{18,2},{3,19},{19,3},{4,20},{20... | collective-permute-start | bytes 2359304 | tf_op jit(solution)/shard_map/ppermute | solution.py:20
  613.8 14.9 %collective-permute-start.30 = (f32[2,384,256]{1,2,0:T(8,128)S(1)}, f32[2,384,256]{1,2,0:T(8,128)S(1)}, u32[]{:S(2)}, u32[]{:S(2)}) collective-permute-start(f32[2,384,256]{1,2,0:T(8,128)S(1)} %maximum_add_fusion.26), channel_id=1, source_target_pairs={{0,4},{4,0},{1,5},{5,1},{2,6},{6,2},{3,7},{7,3},{8,12},{12,8},{9,1... | collective-permute-start | bytes 2359304 | tf_op jit(solution)/shard_map/ppermute | solution.py:20
  702.1 18.8 %collective-permute-start.35 = (f32[2,384,256]{1,2,0:T(8,128)S(1)}, f32[2,384,256]{1,2,0:T(8,128)S(1)}, u32[]{:S(2)}, u32[]{:S(2)}) collective-permute-start(f32[2,384,256]{1,2,0:T(8,128)S(1)} %maximum_add_fusion.30), channel_id=1, source_target_pairs={{0,2},{2,0},{1,3},{3,1},{4,6},{6,4},{5,7},{7,5},{8,10},{10,8},{9,1... | collective-permute-start | bytes 2359304 | tf_op jit(solution)/shard_map/ppermute | solution.py:20
  724.8 19.8 %collective-permute-start.36 = (f32[2,384,256]{1,2,0:T(8,128)S(1)}, f32[2,384,256]{1,2,0:T(8,128)S(1)}, u32[]{:S(2)}, u32[]{:S(2)}) collective-permute-start(f32[2,384,256]{1,2,0:T(8,128)S(1)} %maximum_add_fusion.31), channel_id=1, source_target_pairs={{0,4},{4,0},{1,5},{5,1},{2,6},{6,2},{3,7},{7,3},{8,12},{12,8},{9,1... | collective-permute-start | bytes 2359304 | tf_op jit(solution)/shard_map/ppermute | solution.py:20
  748.5 17.0 %collective-permute-start.37 = (f32[2,384,256]{1,2,0:T(8,128)S(1)}, f32[2,384,256]{1,2,0:T(8,128)S(1)}, u32[]{:S(2)}, u32[]{:S(2)}) collective-permute-start(f32[2,384,256]{1,2,0:T(8,128)S(1)} %maximum_add_fusion.32), channel_id=1, source_target_pairs={{0,8},{8,0},{1,9},{9,1},{2,10},{10,2},{3,11},{11,3},{4,12},{12,4},... | collective-permute-start | bytes 2359304 | tf_op jit(solution)/shard_map/ppermute | solution.py:20
  769.5 17.7 %collective-permute-start.38 = (f32[2,384,256]{1,2,0:T(8,128)S(1)}, f32[2,384,256]{1,2,0:T(8,128)S(1)}, u32[]{:S(2)}, u32[]{:S(2)}) collective-permute-start(f32[2,384,256]{1,2,0:T(8,128)S(1)} %maximum_add_fusion.33), channel_id=1, source_target_pairs={{0,16},{16,0},{1,17},{17,1},{2,18},{18,2},{3,19},{19,3},{4,20},{20... | collective-permute-start | bytes 2359304 | tf_op jit(solution)/shard_map/ppermute | solution.py:20
  791.2 16.7 %collective-permute-start.39 = (f32[2,384,256]{1,2,0:T(8,128)S(1)}, f32[2,384,256]{1,2,0:T(8,128)S(1)}, u32[]{:S(2)}, u32[]{:S(2)}) collective-permute-start(f32[2,384,256]{1,2,0:T(8,128)S(1)} %maximum_add_fusion.34), channel_id=1, source_target_pairs={{0,16},{16,0},{1,17},{17,1},{2,18},{18,2},{3,19},{19,3},{4,20},{20... | collective-permute-start | bytes 2359304 | tf_op jit(solution)/shard_map/ppermute | solution.py:20
  830.3 14.8 %collective-permute-start.41 = (f32[2,384,256]{1,2,0:T(8,128)S(1)}, f32[2,384,256]{1,2,0:T(8,128)S(1)}, u32[]{:S(2)}, u32[]{:S(2)}) collective-permute-start(f32[2,384,256]{1,2,0:T(8,128)S(1)} %maximum_add_fusion.36), channel_id=1, source_target_pairs={{0,4},{4,0},{1,5},{5,1},{2,6},{6,2},{3,7},{7,3},{8,12},{12,8},{9,1... | collective-permute-start | bytes 2359304 | tf_op jit(solution)/shard_map/ppermute | solution.py:20
  (109 other events, 3731.7 us)
where the time goes:
time: 904 us; the launch traced here: 895 us
  waiting for transfers between devices  498 us (55%)
  matrix products  197 us (22%)
  starting transfers between devices  116 us (13%)
  local copies, waits for them, and re-layouts  50 us (6%)
  other arithmetic  30.5 us (3%)
    ppermute x40, waiting for transfers between devices, swapped(): return lax.ppermute(block, axis, route)  469 us
    ppermute x40, starting transfers between devices, swapped(): return lax.ppermute(block, axis, route)  110 us
    dot_general x48, matrix products, complex_apply(): real_real = jnp.matmul(matrix[0], vector[0], precision=highest)  49.6 us
    dot_general x48, matrix products, complex_apply(): imag_imag = jnp.matmul(matrix[1], vector[1], precision=highest)  49.6 us
    dot_general x48, matrix products, complex_apply(): imag_real = jnp.matmul(matrix[1], vector[0], precision=highest)  49.5 us
    dot_general x48, matrix products, complex_apply(): real_imag = jnp.matmul(matrix[0], vector[1], precision=highest)  48.7 us
    ppermute x4, waiting for transfers between devices, from_behind(): return lax.ppermute(x, axis, pairs)  29 us
  transfers between devices with their start and end apart: 44, of which 43 were waited for; matrix products, arithmetic and copies ran while one was open for 1% of the time, Pallas kernels for 0%

commit v1 on v0

v1 whole, which is shorter than its diff:
```python
import jax
import jax.numpy as jnp
from jax import lax
from jax.experimental import pallas as pl
from jax.experimental.pallas import tpu as pltpu
from jax.sharding import PartitionSpec as P

MESH = pl.DeviceIdType.MESH
F32, BF16 = jnp.float32, jnp.bfloat16
WIDTH = 16
HOPS = (1, 2, 3, 4, 4, 3, 2, 1, 0)
LAST = len(HOPS) - 1


def split(x):
    high = x.astype(BF16)
    return high, (x - high.astype(F32)).astype(BF16)


def times(v, high, low):
    blocks, _, width, depth = v.shape
    rows, n = blocks * 2 * width, high.shape[1] // 2
    v_high, v_low = split(v.reshape(rows, depth))
    p = jnp.dot(jnp.concatenate([v_high, v_low], axis=0), high, preferred_element_type=F32)
    r = p[:rows] + p[rows:] + jnp.dot(v_high, low, preferred_element_type=F32)
    r = r.reshape(blocks, 2, width, 2 * n)
    return r[:, 0, :, :n] - r[:, 1, :, n:], r[:, 0, :, n:] + r[:, 1, :, :n]


def kernel(
    src_hbm, inv_hbm, up_hbm, down_hbm, cpl_hbm, row_ref, col_ref, out_ref,
    src, inv, up, down, cpl, wh, wl, ah, al, eh, el, place, pick, take,
    g, g_in, gt, gt_in, s, r, s_last, r_last, sb, rb,
    in_sem, g_send, g_recv, gt_send, gt_recv, send, recv, last_send, last_recv, b_send, b_recv,
):
    size = inv.shape[-1]
    border = cpl.shape[-1]
    columns = src.shape[-1]
    blocks = columns // WIDTH
    levels = up.shape[1]
    layers = lax.axis_size("layer")
    layer, leaf = lax.axis_index("layer"), lax.axis_index("leaf")

    def mirror(bit):
        spread = 1 << bit
        return leaf + (1 - 2 * ((leaf // spread) % 2)) * spread

    below, above = (layer + 1) % layers, (layer + layers - 1) % layers
    partners = [mirror(bit) for bit in range(levels)]

    loads = {}

    def load(name, source, target):
        loads[name] = pltpu.make_async_copy(source, target, in_sem.at[len(loads)])
        loads[name].start()

    load("inv", inv_hbm, inv)
    load("src", src_hbm, src)
    load("up0", up_hbm.at[:, 0], up.at[:, 0])
    load("cpl", cpl_hbm, cpl)
    for bit in range(1, levels):
        load(f"up{bit}", up_hbm.at[:, bit], up.at[:, bit])
    for bit in reversed(range(levels)):
        load(f"down{bit}", down_hbm.at[:, bit], down.at[:, bit])

    barrier = pltpu.get_barrier_semaphore()
    neighbours = [(layer, p) for p in partners]
    neighbours += [(z, q) for z in (below, above) for q in (leaf, partners[0])]
    for device in neighbours:
        pl.semaphore_signal(barrier, inc=1, device_id=device, device_id_type=MESH)

    lane = lax.broadcasted_iota(jnp.int32, (size, size), 1)
    sublane = lax.broadcasted_iota(jnp.int32, (size, size), 0)
    place[...] = jnp.where(sublane == row_ref[...], 1.0, 0.0).astype(BF16)
    pick[...] = jnp.where(lane == col_ref[...], 1.0, 0.0).astype(BF16)

    def prepare(at, matrix):
        for part in range(2):
            high, low = split(matrix[part].T)
            wh[at, :, part * size : (part + 1) * size] = high
            wl[at, :, part * size : (part + 1) * size] = low

    TOP, INV, DOWN0 = 8, 9, 10
    loads["inv"].wait()
    prepare(INV, inv)
    for w in (wh, wl):
        w[INV] = jnp.dot(place[...], w[INV], preferred_element_type=F32).astype(BF16)

    loads["src"].wait()
    for half in range(columns // 128):
        count = 128 // WIDTH
        for part in range(2):
            turned = src[part, :, half * 128 : (half + 1) * 128].T
            g[half * count : (half + 1) * count, part] = turned.reshape(count, WIDTH, size)
    pl.semaphore_wait(barrier, len(neighbours))

    CHUNK = 4
    chunks = blocks // CHUNK

    def g_copy(at):
        part = pl.ds(at * CHUNK, CHUNK)
        return pltpu.make_async_remote_copy(
            g.at[part], g_in.at[part], g_send.at[at], g_recv.at[at],
            device_id=(layer, partners[0]), device_id_type=MESH,
        )

    @pl.loop(0, chunks)
    def _(at):
        part = pl.ds(at * CHUNK, CHUNK)
        real, imag = times(g[part], wh[INV], wl[INV])
        g[part, 0] = real
        g[part, 1] = imag
        g_copy(at).start()

    loads["up0"].wait()
    prepare(TOP, up.at[:, 0])

    gt_copy = pltpu.make_async_remote_copy(
        gt, gt_in, gt_send, gt_recv, device_id=(layer, partners[0]), device_id_type=MESH
    )
    loads["cpl"].wait()

    @pl.when(layer > 0)
    def _():
        turned = jnp.stack([cpl[0].T, cpl[1].T])[None]
        real, imag = times(turned, wh[INV], wl[INV])
        gt[0, 0] = -real[0]
        gt[0, 1] = -imag[0]
        gt_copy.start()

    @pl.loop(0, chunks)
    def _(at):
        part = pl.ds(at * CHUNK, CHUNK)
        g_copy(at).wait()
        real, imag = times(g_in[part], wh[TOP], wl[TOP])
        g[part, 0] = g[part, 0] + real
        g[part, 1] = g[part, 1] + imag

    @pl.when(layer > 0)
    def _():
        gt_copy.wait()
        real, imag = times(gt_in[...], wh[TOP], wl[TOP])
        for row, pair in ((0, (gt[0, 0], gt[0, 1])), (border, (real[0], imag[0]))):
            for part in range(2):
                high, low = split(pair[part])
                ah[row : row + border, part * size : (part + 1) * size] = high
                al[row : row + border, part * size : (part + 1) * size] = low

    def b_copy(block, side):
        target = leaf if side == 0 else partners[0]
        return pltpu.make_async_remote_copy(
            sb.at[block], rb.at[block, side], b_send.at[block, side], b_recv.at[block, side],
            device_id=(below, target), device_id_type=MESH,
        )

    def f_copy(hop, block):
        slot = block % 2
        target = (layer, partners[HOPS[hop]])
        if hop == LAST:
            return pltpu.make_async_remote_copy(
                s_last.at[block], r_last.at[block], last_send.at[slot], last_recv.at[slot],
                device_id=target, device_id_type=MESH,
            )
        return pltpu.make_async_remote_copy(
            s.at[hop, slot], r.at[hop, slot], send.at[hop, slot], recv.at[hop, slot],
            device_id=target, device_id_type=MESH,
        )

    def front(hop, block):
        return s_last.at[block] if hop == LAST else s.at[hop, block % 2]

    def arrived(hop, block):
        return r_last.at[block] if hop == LAST else r.at[hop, block % 2]

    def stage_first(block):
        @pl.when(block >= 2)
        def _():
            f_copy(0, block - 2).wait_send()

        @pl.when(layer == 0)
        def _():
            front(0, block)[...] = g[block]

        @pl.when(layer > 0)
        def _():
            for side in range(2):
                b_copy(block, side).wait_recv()
            v = jnp.concatenate([rb[block, 0], rb[block, 1]], axis=-1)[None]
            real, imag = times(v, ah[...], al[...])
            front(0, block)[0] = g[block, 0] + real[0]
            front(0, block)[1] = g[block, 1] + imag[0]

        f_copy(0, block).start()

    def stage_middle(hop, block):
        @pl.when(block == 0)
        def _():
            name = f"up{hop}" if hop < levels else f"down{HOPS[hop - 1]}"
            loads[name].wait()
            level = HOPS[hop - 1]
            prepare(hop - 1, up.at[:, level] if hop < levels else down.at[:, level])

        @pl.when(block >= 2)
        def _():
            f_copy(hop, block - 2).wait_send()

        f_copy(hop - 1, block).wait_recv()
        real, imag = times(arrived(hop - 1, block)[...][None], wh[hop - 1], wl[hop - 1])
        front(hop, block)[0] = front(hop - 1, block)[0] + real[0]
        front(hop, block)[1] = front(hop - 1, block)[1] + imag[0]
        f_copy(hop, block).start()

    def stage_border(block):
        @pl.when(block == 0)
        def _():
            loads["down0"].wait()
            prepare(DOWN0, down.at[:, 0])
            take[...] = pick[:, size - border :]
            for w, e in ((wh, eh), (wl, el)):
                for part in range(2):
                    e[:, part * border : (part + 1) * border] = jnp.dot(
                        w[DOWN0, :, part * size : (part + 1) * size], take[...], preferred_element_type=F32
                    ).astype(BF16)

        @pl.when(layer < layers - 1)
        def _():
            high, low = split(front(LAST, block)[...].reshape(2 * WIDTH, size))
            own = jnp.dot(jnp.concatenate([high, low], axis=0), take[...], preferred_element_type=F32)
            own = (own[: 2 * WIDTH] + own[2 * WIDTH :]).reshape(2, WIDTH, border)
            f_copy(LAST, block).wait_recv()
            real, imag = times(arrived(LAST, block)[...][None], eh[...], el[...])
            sb[block, 0] = own[0] + real[0]
            sb[block, 1] = own[1] + imag[0]
            for side in range(2):
                b_copy(block, side).start()

        @pl.when(layer == layers - 1)
        def _():
            f_copy(LAST, block).wait_recv()

    def stage_output(half):
        count = 128 // WIDTH
        part = pl.ds(half * count, count)
        real, imag = times(r_last[part], wh[DOWN0], wl[DOWN0])
        for index, add in ((0, real), (1, imag)):
            x = (s_last[part, index] + add).reshape(128, size)
            y = None
            for term in split(x):
                product = jnp.dot(term, pick[...], preferred_element_type=F32)
                y = product if y is None else y + product
            out_ref[index, :, half * 128 : (half + 1) * 128] = y.T

    count = 128 // WIDTH

    @pl.loop(0, blocks + LAST + 1)
    def _(tick):
        for stage in reversed(range(LAST + 2)):
            block = tick - stage

            @pl.when(jnp.logical_and(block >= 0, block < blocks))
            def _():
                if stage == 0:
                    stage_first(block)
                elif stage <= LAST:
                    stage_middle(stage, block)
                else:
                    stage_border(block)

        for half in range(columns // 128):

            @pl.when(tick == LAST + 1 + (half + 1) * count - 1)
            def _():
                stage_output(half)

    for hop in range(LAST + 1):
        for block in (blocks - 2, blocks - 1):
            f_copy(hop, block).wait_send()

    @pl.when(layer < layers - 1)
    def _():
        @pl.loop(0, blocks)
        def _(block):
            for side in range(2):
                b_copy(block, side).wait_send()


def per_device(sources, leaf_inverse, tree_up, tree_down, coupling, index_map):
    size, columns = sources.shape[-2:]
    border = coupling.shape[-1]
    levels = tree_up.shape[3]
    blocks = columns // WIDTH
    operands = (
        sources.reshape(2, size, columns),
        leaf_inverse.reshape(2, size, size),
        tree_up.reshape(2, levels, size, size),
        tree_down.reshape(2, levels, size, size),
        coupling.reshape(2, size, border),
        index_map.reshape(1, size),
        index_map.reshape(size, 1),
    )
    vmem, dma = pltpu.VMEM, pltpu.SemaphoreType.DMA
    wide = 2 * size
    out = pl.pallas_call(
        kernel,
        out_shape=jax.ShapeDtypeStruct((2, size, columns), F32),
        in_specs=[pl.BlockSpec(memory_space=pl.ANY)] * 5 + [pl.BlockSpec(memory_space=pltpu.VMEM)] * 2,
        out_specs=pl.BlockSpec(memory_space=pltpu.VMEM),
        scratch_shapes=[
            vmem((2, size, columns), F32),
            vmem((2, size, size), F32),
            vmem((2, levels, size, size), F32),
            vmem((2, levels, size, size), F32),
            vmem((2, size, border), F32),
            vmem((11, size, wide), BF16),
            vmem((11, size, wide), BF16),
            vmem((2 * border, wide), BF16),
            vmem((2 * border, wide), BF16),
            vmem((size, 2 * border), BF16),
            vmem((size, 2 * border), BF16),
            vmem((size, size), BF16),
            vmem((size, size), BF16),
            vmem((size, border), BF16),
            vmem((blocks, 2, WIDTH, size), F32),
            vmem((blocks, 2, WIDTH, size), F32),
            vmem((1, 2, border, size), F32),
            vmem((1, 2, border, size), F32),
            vmem((LAST, 2, 2, WIDTH, size), F32),
            vmem((LAST, 2, 2, WIDTH, size), F32),
            vmem((blocks, 2, WIDTH, size), F32),
            vmem((blocks, 2, WIDTH, size), F32),
            vmem((blocks, 2, WIDTH, border), F32),
            vmem((blocks, 2, 2, WIDTH, border), F32),
            dma((3 + 2 * levels,)),
            dma((blocks // 4,)),
            dma((blocks // 4,)),
            dma,
            dma,
            dma((LAST, 2)),
            dma((LAST, 2)),
            dma((2,)),
            dma((2,)),
            dma((blocks, 2)),
            dma((blocks, 2)),
        ],
        compiler_params=pltpu.CompilerParams(
            collective_id=0, has_side_effects=True, vmem_limit_bytes=56 * 1024 * 1024
        ),
        name="sweep",
    )(*operands)
    return out.reshape(sources.shape)


def solution(mesh):
    placed = (
        P(None, "layer", "leaf", None, None),
        P(None, "layer", "leaf", None, None),
        P(None, "layer", "leaf", None, None, None),
        P(None, "layer", "leaf", None, None, None),
        P(None, "layer", "leaf", None, None),
        P("layer", "leaf", None),
    )
    return jax.shard_map(
        per_device,
        mesh=mesh,
        in_specs=placed,
        out_specs=P(None, "layer", "leaf", None, None),
        check_vma=False,
    )
```

time: 904 us -> 274 us (0.30)
  waiting for transfers between devices: 498 us -> 0 us
  Pallas kernels: 0 us -> 270 us
  matrix products: 197 us -> 0 us
  starting transfers between devices: 116 us -> 0 us
  local copies, waits for them, and re-layouts: 50 us -> 3.56 us
  other arithmetic: 30.5 us -> 0 us
    ppermute x44 -> x0, waiting for transfers between devices: 498 us -> none  [the longest x40 469 us: swapped(): return lax.ppermute(block, axis, route)]
    pallas_call x0 -> x1, Pallas kernels: none -> 270 us  [per_device(): pl.pallas_call(kernel, out_shape=jax.ShapeDtypeStruct((2, size, columns),...]
    dot_general x192 -> x0, matrix products: 197 us -> none  [the longest x48 49.6 us: complex_apply(): real_real = jnp.matmul(matrix[0], vector[0], precision=highest)]
    ppermute x44 -> x0, starting transfers between devices: 116 us -> none  [the longest x40 110 us: swapped(): return lax.ppermute(block, axis, route)]
    gather x8 -> x0, local copies, waits for them, and re-layouts: 24.4 us -> none  [the longest x4 14.4 us: per_device(): frontal = complex_apply(inverse_local, reduced[:, front_order, :])]
    add x40 -> x0, other arithmetic: 14.4 us -> none  [the longest x20 11.3 us: per_device(): frontal = frontal + complex_apply(downward[:, tree_bit], mirrored)]
  transfers between devices with their start and end apart: 44 -> 0, of which waited for: 43 -> 0; matrix products, arithmetic and copies ran while one was open for 1% -> 0% of each run, Pallas kernels for 0% -> 0%
where the time goes in v1:
time: 274 us; the launch traced here: 273 us
  Pallas kernels  270 us (99%)
  local copies, waits for them, and re-layouts  3.56 us (1%)
    pallas_call x1, Pallas kernels, per_device(): pl.pallas_call(kernel, out_shape=jax.ShapeDtypeStruct((2, size, columns),...  270 us

profile of v1, /device:TPU:97, one launch (start us, length us, event | category | flops | bytes accessed | tf_op | source)
XLA Modules:
  0.0 273.3 jit_solution(11876322262223721046)
XLA Ops:
  0.0 1.5 copy.8.col_ref
  1.5 269.8 %sweep.1 = f32[2,384,256]{2,1,0:T(8,128)} custom-call(f32[2,384,256]{2,1,0:T(8,128)} %bitcast.14, f32[2,384,384]{2,1,0:T(8,128)} %bitcast.13, f32[2,5,384,384]{3,2,1,0:T(8,128)} %bitcast.10, f32[2,5,384,384]{3,2,1,0:T(8,128)} %bitcast.11, f32[2,384,128]{2,1,0:T(8,128)} %bitcast.15, s32[1,384]{1,0:T(1,128)} %bitcast.17, s32[384,1]{1,0:T(8,128)} %copy.8.col_ref), custom_call_target="tpu_custom_call" | custom-call | tf_op jit(solution)/shard_map/sweep/pallas_call | solution.py:303
  271.3 2.1 copy.11

commit v2 on v1

v2 whole, which is shorter than its diff:
```python
import jax
import jax.numpy as jnp
from jax import lax
from jax.experimental import pallas as pl
from jax.experimental.pallas import tpu as pltpu
from jax.sharding import PartitionSpec as P

MESH = pl.DeviceIdType.MESH
F32, BF16 = jnp.float32, jnp.bfloat16
WIDTH = 16
SLOTS = 4
CHUNK = 4

UP1, UP2, UP21, UP3, TURN, TURN2, DOWN3, DOWN1, DOWN2, DOWN12, UP0, INV, DOWN0 = range(13)
LAST = 9

PLAIN = (
    ((), None, False, ((0, 2),)),
    ((0,), UP1, False, ((1, 4),)),
    ((1,), UP2, False, ((3, 8),)),
    ((3,), UP3, False, ((4, 16),)),
    ((4,), TURN, False, ((2, 16),)),
    ((2,), TURN2, False, ((5, 8),)),
    ((5,), DOWN3, False, ((7, 4),)),
    ((7,), DOWN2, False, ((6, 2),)),
    ((6,), DOWN1, False, ((LAST, 1),)),
)
FUSED = (
    ((), None, False, ((1, 4), (0, 2), (2, 6))),
    ((0, 1, 2), UP1, False, ((3, 8),)),
    ((3,), UP3, False, ((4, 16),)),
    ((4,), TURN, True, ((5, 8),)),
    ((5,), DOWN3, False, ((7, 4), (6, 2), (8, 6))),
    ((6, 7, 8), DOWN1, False, ((LAST, 1),)),
)
MASKS = (1, 2, 4, 6, 8, 16)

PLAIN_ORDER = ((0, 0), (9, 12), (5, 8), (6, 9), (8, 11), (7, 10), (2, 3), (4, 6), (1, 1), (3, 4))
FUSED_ORDER = ((0, 0), (2, 3), (3, 4), (4, 5), (6, 7), (1, 1), (5, 6))


def split(x):
    high = x.astype(BF16)
    return high, (x - high.astype(F32)).astype(BF16)


def times(v, high, low):
    blocks, _, width, depth = v.shape
    rows, n = blocks * 2 * width, high.shape[1] // 2
    v_high, v_low = split(v.reshape(rows, depth))
    p = jnp.dot(jnp.concatenate([v_high, v_low], axis=0), high, preferred_element_type=F32)
    r = p[:rows] + p[rows:] + jnp.dot(v_high, low, preferred_element_type=F32)
    r = r.reshape(blocks, 2, width, 2 * n)
    return r[:, 0, :, :n] - r[:, 1, :, n:], r[:, 0, :, n:] + r[:, 1, :, :n]


def kernel(
    src_hbm, inv_hbm, up_hbm, down_hbm, cpl_hbm, row_ref, out_ref,
    src, inv, up, down, cpl, wh, wl, ah, al, eh, el, place, pick, take, far,
    g, g_in, gt, gt_in, s, r, s_last, r_last, sb, rb,
    in_sem, g_send, g_recv, gt_send, gt_recv, far_send, far_recv, send, recv, b_send, b_recv,
):
    size = inv.shape[-1]
    border = cpl.shape[-1]
    columns = src.shape[-1]
    blocks = columns // WIDTH
    levels = up.shape[1]
    layers = lax.axis_size("layer")
    layer, leaf = lax.axis_index("layer"), lax.axis_index("leaf")

    def mirror(mask):
        other = leaf
        for bit in range(levels):
            if mask >> bit & 1:
                other = other + (1 - 2 * ((leaf // (1 << bit)) % 2)) * (1 << bit)
        return other

    below, above = (layer + 1) % layers, (layer + layers - 1) % layers
    partners = {mask: mirror(mask) for mask in MASKS}

    loads = {}

    def load(name, source, target):
        loads[name] = pltpu.make_async_copy(source, target, in_sem.at[len(loads)])
        loads[name].start()

    load("inv", inv_hbm, inv)
    load("src", src_hbm, src)
    load("up0", up_hbm.at[:, 0], up.at[:, 0])

    barrier = pltpu.get_barrier_semaphore()
    neighbours = [(layer, p) for p in partners.values()]
    neighbours += [(z, q) for z in (below, above) for q in (leaf, partners[1])]
    for device in neighbours:
        pl.semaphore_signal(barrier, inc=1, device_id=device, device_id_type=MESH)

    sublane = lax.broadcasted_iota(jnp.int32, (size, size), 0)
    chosen = jnp.where(sublane == row_ref[...], 1.0, 0.0)
    place[...] = chosen.astype(BF16)
    pick[...] = chosen.T.astype(BF16)

    def prepare(at, *matrices):
        for part in range(2):
            total = matrices[0][part]
            for matrix in matrices[1:]:
                total = total + matrix[part]
            high, low = split(total.T)
            wh[at, :, part * size : (part + 1) * size] = high
            wl[at, :, part * size : (part + 1) * size] = low

    loads["inv"].wait()
    prepare(INV, inv)
    for w in (wh, wl):
        w[INV] = jnp.dot(place[...], w[INV], preferred_element_type=F32).astype(BF16)

    loads["src"].wait()
    for bit in (1, 4):
        load(f"up{bit}", up_hbm.at[:, bit], up.at[:, bit])
    load("cpl", cpl_hbm, cpl)
    load("down2", down_hbm.at[:, 2], down.at[:, 2])
    for bit in (2, 3):
        load(f"up{bit}", up_hbm.at[:, bit], up.at[:, bit])
    for bit in (4, 3, 1, 0):
        load(f"down{bit}", down_hbm.at[:, bit], down.at[:, bit])

    for half in range(columns // 128):
        count = 128 // WIDTH
        for part in range(2):
            turned = src[part, :, half * 128 : (half + 1) * 128].T
            g[half * count : (half + 1) * count, part] = turned.reshape(count, WIDTH, size)
    pl.semaphore_wait(barrier, len(neighbours))

    chunks = blocks // CHUNK

    def g_copy(at):
        part = pl.ds(at * CHUNK, CHUNK)
        return pltpu.make_async_remote_copy(
            g.at[part], g_in.at[part], g_send.at[at], g_recv.at[at],
            device_id=(layer, partners[1]), device_id_type=MESH,
        )

    def far_copy(at, source, mask):
        return pltpu.make_async_remote_copy(
            source, far.at[at], far_send.at[at], far_recv.at[at],
            device_id=(layer, partners[mask]), device_id_type=MESH,
        )

    up1_copy = far_copy(0, up.at[:, 1], 4)
    up4_copy = far_copy(1, up.at[:, 4], 16)
    down2_copy = far_copy(2, down.at[:, 2], 2)

    @pl.when(layer > 0)
    def _():
        loads["up1"].wait()
        up1_copy.start()
        loads["up4"].wait()
        up4_copy.start()

    @pl.loop(0, chunks)
    def _(at):
        part = pl.ds(at * CHUNK, CHUNK)
        real, imag = times(g[part], wh[INV], wl[INV])
        g[part, 0] = real
        g[part, 1] = imag
        g_copy(at).start()

    loads["up0"].wait()
    prepare(UP0, up.at[:, 0])

    def couple(at):
        part = pl.ds(at * CHUNK, CHUNK)
        g_copy(at).wait()
        real, imag = times(g_in[part], wh[UP0], wl[UP0])
        g[part, 0] = g[part, 0] + real
        g[part, 1] = g[part, 1] + imag

    def product(at, by, matrix):
        for low_row in range(0, size, 128):
            rows = slice(low_row, low_row + 128)
            v = jnp.stack([matrix[0, :, rows].T, matrix[1, :, rows].T])[None]
            for part, value in enumerate(times(v, wh[by], wl[by])):
                high, low = split(value[0])
                wh[at, rows, part * size : (part + 1) * size] = high
                wl[at, rows, part * size : (part + 1) * size] = low

    def prepare_border():
        loads["down0"].wait()
        prepare(DOWN0, down.at[:, 0])
        take[...] = pick[:, size - border :]
        for w, e in ((wh, eh), (wl, el)):
            for part in range(2):
                e[:, part * border : (part + 1) * border] = jnp.dot(
                    w[DOWN0, :, part * size : (part + 1) * size], take[...], preferred_element_type=F32
                ).astype(BF16)

    gt_copy = pltpu.make_async_remote_copy(
        gt, gt_in, gt_send, gt_recv, device_id=(layer, partners[1]), device_id_type=MESH
    )
    sources_of = {
        UP1: ("up1", up.at[:, 1]), UP2: ("up2", up.at[:, 2]), UP3: ("up3", up.at[:, 3]), TURN: ("up4", up.at[:, 4]),
        TURN2: ("down4", down.at[:, 4]), DOWN3: ("down3", down.at[:, 3]), DOWN1: ("down1", down.at[:, 1]),
        DOWN2: ("down2", down.at[:, 2]),
    }

    @pl.when(layer > 0)
    def _():
        loads["cpl"].wait()
        turned = jnp.stack([cpl[0].T, cpl[1].T])[None]
        real, imag = times(turned, wh[INV], wl[INV])
        gt[0, 0] = -real[0]
        gt[0, 1] = -imag[0]
        gt_copy.start()

        @pl.loop(0, chunks)
        def _(at):
            couple(at)

        gt_copy.wait()
        real, imag = times(gt_in[...], wh[UP0], wl[UP0])
        for row, pair in ((0, (gt[0, 0], gt[0, 1])), (border, (real[0], imag[0]))):
            for part in range(2):
                high, low = split(pair[part])
                ah[row : row + border, part * size : (part + 1) * size] = high
                al[row : row + border, part * size : (part + 1) * size] = low

        for at, (name, matrix) in sources_of.items():
            if at != TURN:
                if at != UP1:
                    loads[name].wait()
                prepare(at, matrix)
        prepare_border()
        up1_copy.wait()
        down2_copy.start()
        product(UP21, UP2, far.at[0])
        up4_copy.wait()
        product(TURN, TURN2, far.at[1])
        prepare(TURN2, up.at[:, 4], down.at[:, 4])
        down2_copy.wait()
        product(DOWN12, DOWN1, far.at[2])

    @pl.when(layer == 0)
    def _():
        loads["cpl"].wait()

    def b_copy(block, side):
        target = partners[1] if side else leaf
        return pltpu.make_async_remote_copy(
            sb.at[block], rb.at[block, side], b_send.at[side], b_recv.at[block, side],
            device_id=(below, target), device_id_type=MESH,
        )

    def sweep(moves, order, plain):
        lags = dict(order)
        final = len(moves)

        def front(stage, block):
            return s_last.at[block] if stage == final - 1 else s.at[stage, block]

        def arrived(lane, block):
            return r_last.at[block] if lane == LAST else r.at[lane, block % SLOTS]

        def f_copy(stage, lane, mask, block):
            return pltpu.make_async_remote_copy(
                front(stage, block), arrived(lane, block), send.at[lane], recv.at[lane, block % SLOTS],
                device_id=(layer, partners[mask]), device_id_type=MESH,
            )

        senders = {lane: (stage, mask) for stage, move in enumerate(moves) for lane, mask in move[3]}

        def receive(lane, block):
            stage, mask = senders[lane]
            f_copy(stage, lane, mask, block).wait_recv()

        def stage_first(block):
            if plain:

                @pl.when(block % CHUNK == 0)
                def _():
                    couple(block // CHUNK)

                front(0, block)[...] = g[block]
            else:
                for side in range(2):
                    b_copy(block, side).wait_recv()
                v = jnp.concatenate([rb[block, 0], rb[block, 1]], axis=-1)[None]
                real, imag = times(v, ah[...], al[...])
                front(0, block)[0] = g[block, 0] + real[0]
                front(0, block)[1] = g[block, 1] + imag[0]

        def stage_middle(stage, block):
            lanes, at, own, _ = moves[stage]
            if plain:

                @pl.when(block == 0)
                def _():
                    name, matrix = sources_of[at]
                    loads[name].wait()
                    prepare(at, matrix)

            for lane in lanes:
                receive(lane, block)
            terms = [front(stage - 1, block)[...]] if own else []
            terms += [arrived(lane, block)[...] for lane in lanes]
            count = len(terms)
            v = terms[0] if count == 1 else jnp.concatenate(terms, axis=-1)
            high = wh[at : at + count].reshape(count * size, 2 * size)
            low = wl[at : at + count].reshape(count * size, 2 * size)
            real, imag = times(v[None], high, low)
            front(stage, block)[0] = front(stage - 1, block)[0] + real[0]
            front(stage, block)[1] = front(stage - 1, block)[1] + imag[0]

        def stage_border(block):
            if plain:

                @pl.when(block == 0)
                def _():
                    prepare_border()

            @pl.when(layer < layers - 1)
            def _():
                high, low = split(front(final - 1, block)[...].reshape(2 * WIDTH, size))
                own = jnp.dot(jnp.concatenate([high, low], axis=0), take[...], preferred_element_type=F32)
                own = (own[: 2 * WIDTH] + own[2 * WIDTH :]).reshape(2, WIDTH, border)
                receive(LAST, block)
                real, imag = times(arrived(LAST, block)[...][None], eh[...], el[...])
                sb[block, 0] = own[0] + real[0]
                sb[block, 1] = own[1] + imag[0]
                for side in range(2):
                    b_copy(block, side).start()

            @pl.when(layer == layers - 1)
            def _():
                receive(LAST, block)

        count = 128 // WIDTH

        def stage_output(half):
            part = pl.ds(half * count, count)
            real, imag = times(r_last[part], wh[DOWN0], wl[DOWN0])
            for index, add in ((0, real), (1, imag)):
                x = (s_last[part, index] + add).reshape(128, size)
                y = None
                for term in split(x):
                    value = jnp.dot(term, pick[...], preferred_element_type=F32)
                    y = value if y is None else y + value
                out_ref[index, :, half * 128 : (half + 1) * 128] = y.T

        @pl.loop(0, blocks + max(lags.values()))
        def _(tick):
            for stage, lag in order:
                block = tick - lag

                @pl.when(jnp.logical_and(block >= 0, block < blocks))
                def _():
                    if stage == final:
                        stage_border(block)
                        return
                    if stage == 0:
                        stage_first(block)
                    else:
                        stage_middle(stage, block)
                    for lane, mask in moves[stage][3]:
                        f_copy(stage, lane, mask, block).start()

            for half in range(columns // 128):

                @pl.when(tick == lags[final] + (half + 1) * count - 1)
                def _():
                    stage_output(half)

        for lane, (stage, mask) in senders.items():
            every = s_last if lane == LAST else s.at[stage]
            pltpu.make_async_remote_copy(
                every, every, send.at[lane], recv.at[0, 0], device_id=(layer, partners[mask]), device_id_type=MESH
            ).wait_send()

    @pl.when(layer == 0)
    def _():
        sweep(PLAIN, PLAIN_ORDER, True)

    @pl.when(layer > 0)
    def _():
        sweep(FUSED, FUSED_ORDER, False)

    @pl.when(layer < layers - 1)
    def _():
        for side in range(2):
            pltpu.make_async_remote_copy(
                sb, sb, b_send.at[side], b_recv.at[0, 0], device_id=(below, leaf), device_id_type=MESH
            ).wait_send()


def per_device(sources, leaf_inverse, tree_up, tree_down, coupling, index_map):
    size, columns = sources.shape[-2:]
    border = coupling.shape[-1]
    levels = tree_up.shape[3]
    blocks = columns // WIDTH
    operands = (
        sources.reshape(2, size, columns),
        leaf_inverse.reshape(2, size, size),
        tree_up.reshape(2, levels, size, size),
        tree_down.reshape(2, levels, size, size),
        coupling.reshape(2, size, border),
        index_map.reshape(1, size),
    )
    vmem, dma = pltpu.VMEM, pltpu.SemaphoreType.DMA
    wide = 2 * size
    out = pl.pallas_call(
        kernel,
        out_shape=jax.ShapeDtypeStruct((2, size, columns), F32),
        in_specs=[pl.BlockSpec(memory_space=pl.ANY)] * 5 + [pl.BlockSpec(memory_space=pltpu.VMEM)],
        out_specs=pl.BlockSpec(memory_space=pltpu.VMEM),
        scratch_shapes=[
            vmem((2, size, columns), F32),
            vmem((2, size, size), F32),
            vmem((2, levels, size, size), F32),
            vmem((2, levels, size, size), F32),
            vmem((2, size, border), F32),
            vmem((13, size, wide), BF16),
            vmem((13, size, wide), BF16),
            vmem((2 * border, wide), BF16),
            vmem((2 * border, wide), BF16),
            vmem((size, 2 * border), BF16),
            vmem((size, 2 * border), BF16),
            vmem((size, size), BF16),
            vmem((size, size), BF16),
            vmem((size, border), BF16),
            vmem((3, 2, size, size), F32),
            vmem((blocks, 2, WIDTH, size), F32),
            vmem((blocks, 2, WIDTH, size), F32),
            vmem((1, 2, border, size), F32),
            vmem((1, 2, border, size), F32),
            vmem((len(PLAIN) - 1, blocks, 2, WIDTH, size), F32),
            vmem((LAST, SLOTS, 2, WIDTH, size), F32),
            vmem((blocks, 2, WIDTH, size), F32),
            vmem((blocks, 2, WIDTH, size), F32),
            vmem((blocks, 2, WIDTH, border), F32),
            vmem((blocks, 2, 2, WIDTH, border), F32),
            dma((4 + 2 * levels,)),
            dma((blocks // CHUNK,)),
            dma((blocks // CHUNK,)),
            dma,
            dma,
            dma((3,)),
            dma((3,)),
            dma((LAST + 1,)),
            dma((LAST + 1, SLOTS)),
            dma((2,)),
            dma((blocks, 2)),
        ],
        compiler_params=pltpu.CompilerParams(
            collective_id=0, has_side_effects=True, vmem_limit_bytes=60 * 1024 * 1024
        ),
        name="sweep",
    )(*operands)
    return out.reshape(sources.shape)


def solution(mesh):
    placed = (
        P(None, "layer", "leaf", None, None),
        P(None, "layer", "leaf", None, None),
        P(None, "layer", "leaf", None, None, None),
        P(None, "layer", "leaf", None, None, None),
        P(None, "layer", "leaf", None, None),
        P("layer", "leaf", None),
    )
    return jax.shard_map(
        per_device,
        mesh=mesh,
        in_specs=placed,
        out_specs=P(None, "layer", "leaf", None, None),
        check_vma=False,
    )
```

time: 274 us -> 222 us (0.81)
  Pallas kernels: 270 us -> 220 us
    pallas_call x1, Pallas kernels: 270 us -> 220 us  [per_device(): pl.pallas_call(kernel, out_shape=jax.ShapeDtypeStruct((2, size, columns),...]
where the time goes in v2:
time: 222 us
  Pallas kernels  220 us (99%)
    pallas_call x1, Pallas kernels, per_device(): pl.pallas_call(kernel, out_shape=jax.ShapeDtypeStruct((2, size, columns),...  220 us

profile of v2, /device:TPU:97, one launch (start us, length us, event | category | flops | bytes accessed | tf_op | source)
XLA Modules:
  0.0 221.8 jit_solution(1616259306908182661)
XLA Ops:
  0.0 219.7 %sweep.1 = f32[2,384,256]{2,1,0:T(8,128)} custom-call(f32[2,384,256]{2,1,0:T(8,128)} %bitcast.13, f32[2,384,384]{2,1,0:T(8,128)} %bitcast.12, f32[2,5,384,384]{3,2,1,0:T(8,128)} %bitcast.9, f32[2,5,384,384]{3,2,1,0:T(8,128)} %bitcast.10, f32[2,384,128]{2,1,0:T(8,128)} %bitcast.14, s32[1,384]{1,0:T(1,128)} %bitcast.15), custom_call_target="tpu_custom_call" | custom-call | tf_op jit(solution)/shard_map/sweep/pallas_call | solution.py:408
  219.7 2.1 copy.9

commit v3 on v2

--- a/solution.py
+++ b/solution.py
@@ -34,6 +34,7 @@
     ((6, 7, 8), DOWN1, False, ((LAST, 1),)),
 )
 MASKS = (1, 2, 4, 6, 8, 16)
+LATE = 3
 
 PLAIN_ORDER = ((0, 0), (9, 12), (5, 8), (6, 9), (8, 11), (7, 10), (2, 3), (4, 6), (1, 1), (3, 4))
 FUSED_ORDER = ((0, 0), (2, 3), (3, 4), (4, 5), (6, 7), (1, 1), (5, 6))
@@ -174,8 +175,8 @@
         g[part, 0] = g[part, 0] + real
         g[part, 1] = g[part, 1] + imag
 
-    def product(at, by, matrix):
-        for low_row in range(0, size, 128):
+    def product(at, by, matrix, parts=(0, 1, 2)):
+        for low_row in (part * (size // 3) for part in parts):
             rows = slice(low_row, low_row + 128)
             v = jnp.stack([matrix[0, :, rows].T, matrix[1, :, rows].T])[None]
             for part, value in enumerate(times(v, wh[by], wl[by])):
@@ -235,8 +236,11 @@
         up4_copy.wait()
         product(TURN, TURN2, far.at[1])
         prepare(TURN2, up.at[:, 4], down.at[:, 4])
-        down2_copy.wait()
-        product(DOWN12, DOWN1, far.at[2])
+
+        @pl.when(layer > 1)
+        def _():
+            down2_copy.wait()
+            product(DOWN12, DOWN1, far.at[2])
 
     @pl.when(layer == 0)
     def _():
@@ -297,17 +301,25 @@
                     loads[name].wait()
                     prepare(at, matrix)
 
+            if stage >= LATE and not plain:
+
+                @pl.when(jnp.logical_and(block == 0, layer == 1))
+                def _():
+                    if stage == LATE:
+                        down2_copy.wait()
+                    product(DOWN12, DOWN1, far.at[2], (stage - LATE,))
+
             for lane in lanes:
                 receive(lane, block)
-            terms = [front(stage - 1, block)[...]] if own else []
+            past = front(stage - 1, block)[...]
+            terms = [past] if own else []
             terms += [arrived(lane, block)[...] for lane in lanes]
-            count = len(terms)
-            v = terms[0] if count == 1 else jnp.concatenate(terms, axis=-1)
-            high = wh[at : at + count].reshape(count * size, 2 * size)
-            low = wl[at : at + count].reshape(count * size, 2 * size)
-            real, imag = times(v[None], high, low)
-            front(stage, block)[0] = front(stage - 1, block)[0] + real[0]
-            front(stage, block)[1] = front(stage - 1, block)[1] + imag[0]
+            total = past[0], past[1]
+            for index, term in enumerate(terms):
+                real, imag = times(term[None], wh[at + index], wl[at + index])
+                total = total[0] + real[0], total[1] + imag[0]
+            front(stage, block)[0] = total[0]
+            front(stage, block)[1] = total[1]
 
         def stage_border(block):
             if plain:

time: 222 us -> 218 us (0.982)
  Pallas kernels: 220 us -> 216 us
    pallas_call x1, Pallas kernels: 220 us -> 216 us  [per_device(): pl.pallas_call(kernel, out_shape=jax.ShapeDtypeStruct((2, size, columns),...]
where the time goes in v3:
time: 218 us
  Pallas kernels  216 us (99%)
    pallas_call x1, Pallas kernels, per_device(): pl.pallas_call(kernel, out_shape=jax.ShapeDtypeStruct((2, size, columns),...  216 us

profile of v3, /device:TPU:97, one launch (start us, length us, event | category | flops | bytes accessed | tf_op | source)
XLA Modules:
  0.0 217.8 jit_solution(4921435020055185039)
XLA Ops:
  0.0 215.8 %sweep.1 = f32[2,384,256]{2,1,0:T(8,128)} custom-call(f32[2,384,256]{2,1,0:T(8,128)} %bitcast.13, f32[2,384,384]{2,1,0:T(8,128)} %bitcast.12, f32[2,5,384,384]{3,2,1,0:T(8,128)} %bitcast.9, f32[2,5,384,384]{3,2,1,0:T(8,128)} %bitcast.10, f32[2,384,128]{2,1,0:T(8,128)} %bitcast.14, s32[1,384]{1,0:T(1,128)} %bitcast.15), custom_call_target="tpu_custom_call" | custom-call | tf_op jit(solution)/shard_map/sweep/pallas_call | solution.py:420
  215.8 2.1 copy.9

commit v4 on v3

--- a/solution.py
+++ b/solution.py
@@ -157,13 +157,16 @@
         loads["up4"].wait()
         up4_copy.start()
 
-    @pl.loop(0, chunks)
-    def _(at):
+    def lead(at):
         part = pl.ds(at * CHUNK, CHUNK)
         real, imag = times(g[part], wh[INV], wl[INV])
         g[part, 0] = real
         g[part, 1] = imag
         g_copy(at).start()
+
+    @pl.loop(0, jnp.where(layer == 0, 1, chunks))
+    def _(at):
+        lead(at)
 
     loads["up0"].wait()
     prepare(UP0, up.at[:, 0])
@@ -281,6 +284,10 @@
                 @pl.when(block % CHUNK == 0)
                 def _():
                     couple(block // CHUNK)
+
+                @pl.when(jnp.logical_and(block % CHUNK == 1, block < blocks - CHUNK))
+                def _():
+                    lead(block // CHUNK + 1)
 
                 front(0, block)[...] = g[block]
             else:

time: 218 us -> 217 us (level)
  no operation moved by 1% of the time
where the time goes in v4:
time: 217 us
  Pallas kernels  215 us (99%)
    pallas_call x1, Pallas kernels, per_device(): pl.pallas_call(kernel, out_shape=jax.ShapeDtypeStruct((2, size, columns),...  215 us

profile of v4, /device:TPU:97, one launch (start us, length us, event | category | flops | bytes accessed | tf_op | source)
XLA Modules:
  0.0 217.1 jit_solution(4502251480202018512)
XLA Ops:
  0.0 215.1 %sweep.1 = f32[2,384,256]{2,1,0:T(8,128)} custom-call(f32[2,384,256]{2,1,0:T(8,128)} %bitcast.13, f32[2,384,384]{2,1,0:T(8,128)} %bitcast.12, f32[2,5,384,384]{3,2,1,0:T(8,128)} %bitcast.9, f32[2,5,384,384]{3,2,1,0:T(8,128)} %bitcast.10, f32[2,384,128]{2,1,0:T(8,128)} %bitcast.14, s32[1,384]{1,0:T(1,128)} %bitcast.15), custom_call_target="tpu_custom_call" | custom-call | tf_op jit(solution)/shard_map/sweep/pallas_call | solution.py:427
  215.1 2.1 copy.9
